TPU v7x, 256 devices: a whole 4x4x8 slice. The times are simulated.
256 devices in a mesh: outer: 8 (over z), inner: 32 (over x, y, core).
Axes of the slice: x: 4, y: 4, z: 8, core: 2. Of those that a mesh axis runs over, the one named last changes fastest.
Arguments:
- query: bfloat16 [32768, 16, 128], P(('outer', 'inner')), may hold values from -6 to 6
- key_inputs: bfloat16 [32768, 16, 128], P(('outer', 'inner')), may hold values from -6 to 6
- value_inputs: bfloat16 [32768, 16, 128], P(('outer', 'inner')), may hold values from -6 to 6
- output_gradient: bfloat16 [32768, 16, 128], P(('outer', 'inner')), may hold values from -6 to 6
Outputs:
- grad_query: bfloat16 [32768, 16, 128], P(('outer', 'inner'))
- grad_key: bfloat16 [32768, 16, 128], P(('outer', 'inner'))
- grad_value: bfloat16 [32768, 16, 128], P(('outer', 'inner'))
All inputs are finite; a program needn't handle non-finite values.
Results may differ from a plain program's by a relative error of at most 0.005.
Values sent between devices are 32-bit elements; how exact they have to be, the bound alone decides.
A program may use at most 192 MiB of HBM per device.

v0:
```python
import jax
import jax.numpy as jnp
from jax import lax
from jax.sharding import PartitionSpec as P


def carried_in(x, axis, combine, identity):
    count, place = (lax.axis_size(axis), lax.axis_index(axis))
    everything = jax.tree.map(lambda part: lax.all_gather(part, axis), x)
    start = jax.tree.map(
        lambda part, zero: jnp.broadcast_to(jnp.asarray(zero, part.dtype), part.shape), x, identity
    )

    def step(k, before):
        reached = k < place
        new = combine(before, jax.tree.map(lambda part: part[k], everything))
        return jax.tree.map(lambda a, b: jnp.where(reached, a, b), new, before)

    return lax.fori_loop(0, count, step, start)


def add_states(earlier, later):
    return jax.tree.map(lambda a, b: a + b, earlier, later)


def carry_states(states):
    empty = jax.tree.map(jnp.zeros_like, states)
    within = carried_in(states, "inner", add_states, empty)
    totals = lax.psum((states[0], states[1]), "inner")
    groups = carried_in(totals, "outer", add_states, empty)
    return (add_states(within, groups), totals)


def body(query, key_inputs, value_inputs, output_gradient):
    rows_here = query.shape[0]
    head_size = query.shape[2]
    total_rows = rows_here * lax.axis_size("outer") * lax.axis_size("inner")
    scale = (head_size * total_rows) ** (-0.5)
    key_value_state = jnp.einsum(
        "xfw,xfs->fws", key_inputs, value_inputs, preferred_element_type=jnp.float32
    )
    query_output_state = jnp.einsum(
        "xfw,xfs->fws", query, output_gradient, preferred_element_type=jnp.float32
    )
    carried, unused = carry_states((key_value_state, query_output_state))
    prefix_running, before = carried
    total = lax.psum(query_output_state, ("outer", "inner"))
    suffix = total - before - query_output_state
    rows = lax.broadcasted_iota(jnp.int32, (rows_here, rows_here), 0)
    cols = lax.broadcasted_iota(jnp.int32, (rows_here, rows_here), 1)
    causal = (cols <= rows)[None]
    score = jnp.einsum("thk,shk->hts", query, key_inputs, preferred_element_type=jnp.float32)
    score_low = jnp.where(causal, score, jnp.float32(0.0)).astype(jnp.bfloat16)
    dprob = jnp.einsum(
        "thk,shk->hts", output_gradient, value_inputs, preferred_element_type=jnp.float32
    )
    dprob_low = jnp.where(causal, dprob, jnp.float32(0.0)).astype(jnp.bfloat16)
    prefix_lower = prefix_running.astype(jnp.bfloat16)
    suffix_lower = suffix.astype(jnp.bfloat16)
    grad_q = jnp.einsum("hts,shk->thk", dprob_low, key_inputs, preferred_element_type=jnp.float32)
    grad_q = grad_q + jnp.einsum(
        "swx,wmx->swm", output_gradient, prefix_lower, preferred_element_type=jnp.float32
    )
    key_gradient = jnp.einsum("hts,thk->shk", dprob_low, query, preferred_element_type=jnp.float32)
    key_gradient = key_gradient + jnp.einsum(
        "ujt,jit->uji", value_inputs, suffix_lower, preferred_element_type=jnp.float32
    )
    value_gradient = jnp.einsum(
        "hts,thv->shv", score_low, output_gradient, preferred_element_type=jnp.float32
    )
    value_gradient = value_gradient + jnp.einsum(
        "diw,iwf->dif", key_inputs, suffix_lower, preferred_element_type=jnp.float32
    )
    return (
        (scale * grad_q).astype(jnp.bfloat16),
        (scale * key_gradient).astype(jnp.bfloat16),
        (scale * value_gradient).astype(jnp.bfloat16),
    )


def solution(mesh):
    return jax.shard_map(
        body,
        mesh=mesh,
        in_specs=(
            P(("outer", "inner"), None, None),
            P(("outer", "inner"), None, None),
            P(("outer", "inner"), None, None),
            P(("outer", "inner"), None, None),
        ),
        out_specs=(
            P(("outer", "inner"), None, None),
            P(("outer", "inner"), None, None),
            P(("outer", "inner"), None, None),
        ),
        check_vma=False,
    )
```

profile of v0, /device:TPU:1, one launch (start us, length us, event | category | flops | bytes accessed | tf_op | source)
XLA Modules:
  0.0 674.6 jit_solution(18419986645261611534)
XLA Ops:
  10.9 2.5 fusion.15
  13.4 121.0 %all-gather.11.cloned.1.call-done = f32[512,128,128]{2,1,0:T(8,128)} async-done(((f32[16,128,128]{2,1,0:T(8,128)}), f32[512,128,128]{2,1,0:T(8,128)}) %all-gather.11.cloned.1.call-update) | async-done | bytes 33554448 | tf_op jit(solution)/shard_map/all_gather | solution.py:9
  136.0 119.1 %all-reduce.6.cloned.1.call-done = (f32[1,16,128,128]{3,2,1,0:T(8,128)}, f32[1,16,128,128]{3,2,1,0:T(8,128)}) async-done(((f32[1,16,128,128]{3,2,1,0:T(8,128)}, f32[1,16,128,128]{3,2,1,0:T(8,128)}), (f32[1,16,128,128]{3,2,1,0:T(8,128)}, f32[1,16,128,128]{3,2,1,0:T(8,128)})) %all-reduce.6.cloned.1.call-update) | async-done | bytes 2097168 | tf_op jit(solution)/shard_map/psum | solution.py:29
  256.4 2.7 convolution_bitcast_fusion.1
  260.6 2.4 convolution_bitcast_fusion.3
  263.0 2.3 convolution_bitcast_fusion.5
  265.3 112.2 %all-gather.13.cloned.1.call-done = f32[512,128,128]{2,1,0:T(8,128)} async-done(((f32[16,128,128]{2,1,0:T(8,128)}), f32[512,128,128]{2,1,0:T(8,128)}) %all-gather.13.cloned.1.call-update) | async-done | bytes 33554448 | tf_op jit(solution)/shard_map/all_gather | solution.py:9
  377.5 130.9 %while.32 = (s32[]{:T(128)}, f32[16,128,128]{2,1,0:T(8,128)}, f32[16,128,128]{2,1,0:T(8,128)}, s32[]{:T(128)}, f32[32,16,128,128]{3,2,1,0:T(8,128)}, /*index=5*/f32[32,16,128,128]{3,2,1,0:T(8,128)}, s32[]{:T(128)}, s32[]{:T(128)}) while((s32[]{:T(128)}, f32[16,128,128]{2,1,0:T(8,128)}, f32[16,128,128]{2,1,0:T(8,128)}, s32[]{:T(128)}, ...), condition=%wide.region_1.2_spmd.clone, body=%wide.region_0.1_spmd.clone.sunk | while | flops 1572868 | bytes 6291565 | solution.py:19
  377.5 3.5 add_select_fusion.6
  381.0 4.1 add_select_fusion.6
  385.1 4.1 add_select_fusion.6
  389.2 4.4 add_select_fusion.6
  393.6 4.1 add_select_fusion.6
  397.6 4.1 add_select_fusion.6
  401.7 4.1 add_select_fusion.6
  405.8 4.1 add_select_fusion.6
  409.9 4.1 add_select_fusion.6
  414.0 4.1 add_select_fusion.6
  418.1 4.1 add_select_fusion.6
  422.2 4.1 add_select_fusion.6
  426.3 4.1 add_select_fusion.6
  430.4 4.1 add_select_fusion.6
  434.5 4.1 add_select_fusion.6
  438.6 4.1 add_select_fusion.6
  442.7 4.1 add_select_fusion.6
  446.8 4.1 add_select_fusion.6
  450.9 4.1 add_select_fusion.6
  455.0 4.1 add_select_fusion.6
  459.1 4.1 add_select_fusion.6
  463.2 4.1 add_select_fusion.6
  467.3 4.1 add_select_fusion.6
  471.3 4.1 add_select_fusion.6
  475.4 4.1 add_select_fusion.6
  479.5 4.1 add_select_fusion.6
  483.6 4.4 add_select_fusion.6
  488.0 4.1 add_select_fusion.6
  492.0 4.1 add_select_fusion.6
  496.1 4.1 add_select_fusion.6
  500.2 4.1 add_select_fusion.6
  504.3 4.1 add_select_fusion.6
  508.4 59.1 %all-gather.9.cloned.1.call-done = f32[8,16,128,128]{3,2,1,0:T(8,128)} async-done(((f32[1,16,128,128]{3,2,1,0:T(8,128)}), f32[8,16,128,128]{3,2,1,0:T(8,128)}) %all-gather.9.cloned.1.call-update) | async-done | bytes 8388624 | tf_op jit(solution)/shard_map/all_gather | solution.py:9
  567.5 18.2 %while.33 = (s32[]{:T(128)}, f32[16,128,128]{2,1,0:T(8,128)S(1)}, f32[16,128,128]{2,1,0:T(8,128)S(1)}, s32[]{:T(128)}, f32[8,16,128,128]{3,2,1,0:T(8,128)}, /*in...) while((s32[]{:T(128)}, f32[16,128,128]{2,1,0:T(8,128)S(1)}, f32[16,128,128]{2,1,0:T(8,128)S(1)}, ...), condition=%wide.region_5.6_spmd.clone, body=%wide.region_4.5_spmd.clone.sunk | while | flops 1572868 | bytes 6291565 | solution.py:19
  574.4 2.3 add_select_fusion.7
  576.7 2.3 add_select_fusion.7
  578.9 2.3 add_select_fusion.7
  581.2 2.3 add_select_fusion.7
  583.5 2.3 add_select_fusion.7
  585.8 70.7 %all-reduce.4.cloned.1.call-done = f32[16,128,128]{2,1,0:T(8,128)} async-done(((f32[16,128,128]{2,1,0:T(8,128)}), f32[16,128,128]{2,1,0:T(8,128)}) %all-reduce.4.cloned.1.call-update) | async-done | bytes 1048592 | tf_op jit(solution)/shard_map/psum | solution.py:47
  (35 shorter events, 24.8 us)
Async XLA Ops:
  8.0 1.6 copy-start
  8.0 126.5 %all-gather.11.cloned.1.call-start = ((), (), s32[]{:S(2)}) async-start(), calls=%async_computation.3 | async-start | bytes 34603008 | tf_op jit(solution)/shard_map/all_gather | solution.py:9
  134.5 120.6 %all-reduce.6.cloned.1.call-start = ((), (), s32[]{:S(2)}) async-start(), calls=%async_computation.5 | async-start | bytes 4194304 | tf_op jit(solution)/shard_map/psum | solution.py:29
  135.2 242.3 %all-gather.13.cloned.1.call-start = ((), (), s32[]{:S(2)}) async-start(), calls=%async_computation.4 | async-start | bytes 34603008 | tf_op jit(solution)/shard_map/all_gather | solution.py:9
  136.0 372.5 %all-gather.7.cloned.1.call-start = ((), (), s32[]{:S(2)}) async-start(), calls=%async_computation | async-start | bytes 9437184 | tf_op jit(solution)/shard_map/all_gather | solution.py:9
  255.1 312.4 %all-gather.9.cloned.1.call-start = ((), (), s32[]{:S(2)}) async-start(), calls=%async_computation.1 | async-start | bytes 9437184 | tf_op jit(solution)/shard_map/all_gather | solution.py:9
  255.7 400.7 %all-reduce.4.cloned.1.call-start = ((), (), s32[]{:S(2)}) async-start(), calls=%async_computation.2 | async-start | bytes 2097152 | tf_op jit(solution)/shard_map/psum | solution.py:47
  377.5 281.0 %copy-start.1 = (bf16[128,16,128]{2,1,0:T(8,128)(2,1)S(1)}, bf16[128,16,128]{2,1,0:T(8,128)(2,1)}, u32[]{:S(2)}) copy-start(bf16[128,16,128]{2,1,0:T(8,128)(2,1)} %param.9) | copy-start | bytes 1572868
Sparse Core Ops, SparseCore 0:
  11.4 123.0 all-gather.10
  138.6 116.4 all-reduce.5
  257.7 119.8 all-gather.12
  379.2 93.5 all-gather.6
  474.4 93.0 all-gather.8
Sparse Core Ops, SparseCore 1:
  261.7 394.7 all-reduce.3
where the time goes:
time: 676 us; the launch traced here: 675 us
  waiting for transfers between devices  485 us (72%)
  other arithmetic  151 us (22%)
  matrix products  18.2 us (3%)
  between operations  15.3 us (2%)
    all_gather x4, waiting for transfers between devices, carried_in(): everything = jax.tree.map(lambda part: lax.all_gather(part, axis), x)  292 us
    select_n x40, other arithmetic, step(): return jax.tree.map(lambda a, b: jnp.where(reached, a, b), new, before)  149 us
    psum x1, waiting for transfers between devices, carry_states(): totals = lax.psum((states[0], states[1]), 'inner')  119 us
    psum x1, waiting for transfers between devices, body(): total = lax.psum(query_output_state, ('outer', 'inner'))  70.7 us
  transfers between devices with their start and end apart: 6, of which 5 were waited for; matrix products, arithmetic and copies ran while one was open for 24% of the time, Pallas kernels for 0%

commit v1 on v0

v1 whole, which is shorter than its diff:
```python
import functools

import jax
import jax.numpy as jnp
from jax import lax
from jax.experimental import pallas as pl
from jax.experimental.pallas import tpu as pltpu
from jax.sharding import PartitionSpec as P

MESH = pl.DeviceIdType.MESH
GROUPS = 2

PAIR, UP, ALONG, DOWN, BACK = range(5)


def nn(a, b):
    return lax.dot_general(a, b, (((1,), (0,)), ((), ())), preferred_element_type=jnp.float32)


def nt(a, b):
    return lax.dot_general(a, b, (((1,), (1,)), ((), ())), preferred_element_type=jnp.float32)


def tn(a, b):
    return lax.dot_general(a, b, (((0,), (0,)), ((), ())), preferred_element_type=jnp.float32)


def kernel(
    dims, scale,
    q_ref, k_ref, v_ref, g_ref, dq_ref, dk_ref, dv_ref,
    qt, kt, vt, gt, acc, res, own, pair, chip, got, plane, along, down, base, back, final,
    send, recv,
):
    nz, nxy, groups = dims
    heads, tok, dim = qt.shape
    per = heads // groups
    half = per // 2
    rows = half * dim
    r = rows // nxy
    z = lax.axis_index("outer")
    inner = lax.axis_index("inner")
    xy, core = inner // 2, inner % 2

    def there(dz, dxy, dcore):
        return (lax.rem(z + dz, nz), lax.rem(xy + dxy, nxy) * 2 + lax.rem(core + dcore, 2))

    partners = [there(0, 0, 1)]
    partners += [there(0, k, 0) for k in range(1, nxy)]
    partners += [there(k, 0, 0) for k in range(1, nz)]
    barrier = pltpu.get_barrier_semaphore()
    for who in partners:
        pl.semaphore_signal(barrier, inc=1, device_id=who, device_id_type=MESH)

    def remote(src, dst, stage, g, who):
        return pltpu.make_async_remote_copy(
            src_ref=src, dst_ref=dst, send_sem=send.at[stage, g], recv_sem=recv.at[stage, g],
            device_id=who, device_id_type=MESH,
        )

    def arrived(ref, stage, g):
        pltpu.make_async_copy(ref, ref, recv.at[stage, g]).wait()

    def left(ref, stage, g):
        pltpu.make_async_copy(ref, ref, send.at[stage, g]).wait()

    kt[...] = jnp.swapaxes(k_ref[...], 0, 1)
    vt[...] = jnp.swapaxes(v_ref[...], 0, 1)
    qt[...] = jnp.swapaxes(q_ref[...], 0, 1)
    gt[...] = jnp.swapaxes(g_ref[...], 0, 1)

    def states(g):
        for part in range(2):
            def one(j, _, part=part):
                h = g * per + part * half + j
                at = pl.ds(pl.multiple_of(j * dim, dim), dim)
                own[g, part, 0, at] = tn(kt[h], vt[h])
                own[g, part, 1, at] = tn(qt[h], gt[h])
                return 0
            lax.fori_loop(0, half, one, 0, unroll=2)

    def pair_start(g):
        remote(own.at[g, 1 - core], pair.at[g], PAIR, g, there(0, 0, 1)).start()

    def up_start(g):
        arrived(pair.at[g], PAIR, g)
        for s in range(2):
            total = own[g, core, s] + pair[g, s]
            chip[g, :, s] = total.reshape(nxy, r, dim)
        pltpu.make_async_copy(chip.at[g, xy], got.at[g, xy], recv.at[UP, g]).start()
        for k in range(1, nxy):
            who = lax.rem(xy + k, nxy)
            remote(chip.at[g, who], got.at[g, xy], UP, g, there(0, k, 0)).start()

    def along_start(g):
        arrived(got.at[g], UP, g)
        plane[g] = jnp.sum(got[g], axis=0)
        for k in range(1, nz):
            later = lax.rem(z + k, nz) > z
            remote(plane.at[g, jnp.where(later, 0, 1)], along.at[g, k - 1], ALONG, g, there(k, 0, 0)).start()

    def down_start(g):
        arrived(along.at[g], ALONG, g)
        before = jnp.zeros((r, dim), jnp.float32)
        after = jnp.zeros((r, dim), jnp.float32)
        for k in range(1, nz):
            value = along[g, k - 1]
            before = before + jnp.where(k <= z, value, 0.0)
            after = after + jnp.where(k > z, value, 0.0)
        for i in range(nxy):
            down[g, i, 0] = before
            before = before + got[g, i, 0]
        for i in reversed(range(nxy)):
            down[g, i, 1] = after
            after = after + got[g, i, 1]
        pltpu.make_async_copy(down.at[g, xy], base.at[g, xy], recv.at[DOWN, g]).start()
        for k in range(1, nxy):
            who = lax.rem(xy + k, nxy)
            remote(down.at[g, who], base.at[g, xy], DOWN, g, there(0, k, 0)).start()

    def back_start(g):
        arrived(base.at[g], DOWN, g)
        first = core == 0
        before = base[g, :, 0].reshape(rows, dim)
        after = base[g, :, 1].reshape(rows, dim)
        back[g, 0] = before + jnp.where(first, own[g, core, 0], 0.0)
        back[g, 1] = after + jnp.where(first, 0.0, own[g, core, 1])
        remote(back.at[g], final.at[g, 1], BACK, g, there(0, 0, 1)).start()
        final[g, 0, 0] = before + jnp.where(first, 0.0, pair[g, 0])
        final[g, 0, 1] = after + jnp.where(first, pair[g, 1], 0.0)

    def local(h, _):
        at = lax.broadcasted_iota(jnp.int32, (tok, tok), 0)
        to = lax.broadcasted_iota(jnp.int32, (tok, tok), 1)
        q, k, v, d = qt[h], kt[h], vt[h], gt[h]
        dprob = jnp.where(to <= at, nt(d, v), 0.0).astype(jnp.bfloat16)
        dprob_t = jnp.where(at <= to, nt(v, d), 0.0).astype(jnp.bfloat16)
        score_t = jnp.where(at <= to, nt(k, q), 0.0).astype(jnp.bfloat16)
        acc[0, h] = nn(dprob, k)
        acc[1, h] = nn(dprob_t, q)
        acc[2, h] = nn(score_t, d)
        return 0

    def finish(g, which):
        part = core if which == 0 else 1 - core

        def one(j, _):
            h = g * per + part * half + j
            at = pl.ds(pl.multiple_of(j * dim, dim), dim)
            before = final[g, which, 0, at].astype(jnp.bfloat16)
            after = final[g, which, 1, at].astype(jnp.bfloat16)
            res[0, h] = (scale * (acc[0, h] + nt(gt[h], before))).astype(jnp.bfloat16)
            res[1, h] = (scale * (acc[1, h] + nt(vt[h], after))).astype(jnp.bfloat16)
            res[2, h] = (scale * (acc[2, h] + nn(kt[h], after))).astype(jnp.bfloat16)
            return 0

        lax.fori_loop(0, half, one, 0, unroll=2)

    def local_group(g):
        lax.fori_loop(g * per, (g + 1) * per, local, 0, unroll=2)

    states(0)
    pl.semaphore_wait(barrier, len(partners))
    pair_start(0)
    for g in range(1, groups):
        states(g)
        pair_start(g)
        up_start(g - 1)
    up_start(groups - 1)
    for g in range(groups):
        local_group(g)
    for g in range(groups):
        along_start(g)
        if g >= 1:
            down_start(g - 1)
    down_start(groups - 1)
    for g in range(groups):
        back_start(g)
        finish(g, 0)
        arrived(final.at[g, 1], BACK, g)
        finish(g, 1)
    dq_ref[...] = jnp.swapaxes(res[0], 0, 1)
    dk_ref[...] = jnp.swapaxes(res[1], 0, 1)
    dv_ref[...] = jnp.swapaxes(res[2], 0, 1)

    for g in range(groups):
        left(pair.at[g], PAIR, g)
        left(chip.at[g, pl.ds(0, nxy - 1)], UP, g)
        left(along.at[g], ALONG, g)
        left(down.at[g, pl.ds(0, nxy - 1)], DOWN, g)
        left(back.at[g], BACK, g)


def solution(mesh):
    nz, nxy = mesh.shape["outer"], mesh.shape["inner"] // 2
    groups = GROUPS

    def step(q, k, v, g):
        tok, heads, dim = q.shape
        scale = (dim * tok * mesh.size) ** -0.5
        rows = heads // groups // 2 * dim
        r = rows // nxy
        f32, low = jnp.float32, jnp.bfloat16
        vmem = pl.BlockSpec(memory_space=pltpu.VMEM)
        return pl.pallas_call(
            functools.partial(kernel, (nz, nxy, groups), scale),
            out_shape=[jax.ShapeDtypeStruct((tok, heads, dim), low)] * 3,
            in_specs=[vmem] * 4,
            out_specs=[vmem] * 3,
            scratch_shapes=[
                pltpu.VMEM((heads, tok, dim), low),
                pltpu.VMEM((heads, tok, dim), low),
                pltpu.VMEM((heads, tok, dim), low),
                pltpu.VMEM((heads, tok, dim), low),
                pltpu.VMEM((3, heads, tok, dim), f32),
                pltpu.VMEM((3, heads, tok, dim), low),
                pltpu.VMEM((groups, 2, 2, rows, dim), f32),
                pltpu.VMEM((groups, 2, rows, dim), f32),
                pltpu.VMEM((groups, nxy, 2, r, dim), f32),
                pltpu.VMEM((groups, nxy, 2, r, dim), f32),
                pltpu.VMEM((groups, 2, r, dim), f32),
                pltpu.VMEM((groups, nz - 1, r, dim), f32),
                pltpu.VMEM((groups, nxy, 2, r, dim), f32),
                pltpu.VMEM((groups, nxy, 2, r, dim), f32),
                pltpu.VMEM((groups, 2, rows, dim), f32),
                pltpu.VMEM((groups, 2, 2, rows, dim), f32),
                pltpu.SemaphoreType.DMA((5, groups)),
                pltpu.SemaphoreType.DMA((5, groups)),
            ],
            compiler_params=pltpu.CompilerParams(
                collective_id=0, has_side_effects=True, vmem_limit_bytes=48 * 2**20
            ),
        )(q, k, v, g)

    spec = P(("outer", "inner"), None, None)
    return jax.shard_map(
        step, mesh=mesh, in_specs=(spec,) * 4, out_specs=(spec,) * 3, check_vma=False
    )
```

time: 676 us -> 55.1 us (0.08)
  waiting for transfers between devices: 485 us -> 0 us
  other arithmetic: 151 us -> 0 us
  Pallas kernels: 0 us -> 47.6 us
  matrix products: 18.2 us -> 0 us
  between operations: 15.3 us -> 0.65 us
    all_gather x4 -> x0, waiting for transfers between devices: 292 us -> none  [carried_in(): everything = jax.tree.map(lambda part: lax.all_gather(part, axis), x)]
    psum x2 -> x0, waiting for transfers between devices: 190 us -> none  [the longest x1 119 us: carry_states(): totals = lax.psum((states[0], states[1]), 'inner')]
    select_n x40 -> x0, other arithmetic: 149 us -> none  [step(): return jax.tree.map(lambda a, b: jnp.where(reached, a, b), new, before)]
    pallas_call x0 -> x1, Pallas kernels: none -> 47.6 us  [step(): pl.pallas_call(functools.partial(kernel, (nz, nxy, groups), scale), out_s...]
    dot_general x9 -> x0, matrix products: 18.2 us -> none  [the longest x1 2.69 us: body(): jnp.einsum('hts,thv->shv', score_low, output_gradient, preferred_element_...]
  transfers between devices with their start and end apart: 6 -> 0, of which waited for: 5 -> 0; matrix products, arithmetic and copies ran while one was open for 24% -> 0% of each run, Pallas kernels for 0% -> 0%
where the time goes in v1:
time: 55.1 us; the launch traced here: 54.8 us
  Pallas kernels  47.6 us (86%)
  local copies, waits for them, and re-layouts  6.54 us (12%)
  between operations  0.65 us (1%)
    pallas_call x1, Pallas kernels, step(): pl.pallas_call(functools.partial(kernel, (nz, nxy, groups), scale), out_s...  47.6 us
    unnamed x11, local copies, waits for them, and re-layouts  6.54 us

profile of v1, /device:TPU:1, one launch (start us, length us, event | category | flops | bytes accessed | tf_op | source)
XLA Modules:
  0.0 54.8 jit_solution(9523665535666136018)
XLA Ops:
  0.6 0.0 copy-start
  0.6 1.0 %copy-done = bf16[128,16,128]{2,1,0:T(8,128)(2,1)S(1)} copy-done((bf16[128,16,128]{2,1,0:T(8,128)(2,1)S(1)}, bf16[128,16,128]{2,1,0:T(8,128)(2,1)}, u32[]{:S(2)}) %copy-start) | copy-done | bytes 524312
  1.7 0.0 copy-start.1
  1.7 1.0 %copy-done.1 = bf16[128,16,128]{2,1,0:T(8,128)(2,1)S(1)} copy-done((bf16[128,16,128]{2,1,0:T(8,128)(2,1)S(1)}, bf16[128,16,128]{2,1,0:T(8,128)(2,1)}, u32[]{:S(2)}) %copy-start.1) | copy-done | bytes 524312
  2.7 0.0 copy-start.2
  2.7 1.0 %copy-done.2 = bf16[128,16,128]{2,1,0:T(8,128)(2,1)S(1)} copy-done((bf16[128,16,128]{2,1,0:T(8,128)(2,1)S(1)}, bf16[128,16,128]{2,1,0:T(8,128)(2,1)}, u32[]{:S(2)}) %copy-start.2) | copy-done | bytes 524312
  3.8 0.0 copy-start.3
  3.8 1.0 %copy-done.3 = bf16[128,16,128]{2,1,0:T(8,128)(2,1)S(1)} copy-done((bf16[128,16,128]{2,1,0:T(8,128)(2,1)S(1)}, bf16[128,16,128]{2,1,0:T(8,128)(2,1)}, u32[]{:S(2)}) %copy-start.3) | copy-done | bytes 524312
  4.8 47.6 %shard_map.67 = (bf16[128,16,128]{2,1,0:T(8,128)(2,1)S(1)}, bf16[128,16,128]{2,1,0:T(8,128)(2,1)S(1)}, bf16[128,16,128]{2,1,0:T(8,128)(2,1)S(1)}) custom-call(bf16[128,16,128]{2,1,0:T(8,128)(2,1)S(1)} %copy-done, bf16[128,16,128]{2,1,0:T(8,128)(2,1)S(1)} %copy-done.1, bf16[128,16,128]{2,1,0:T(8,128)(2,1)S(1)} %copy-done.2, bf16[128,16,128]{2,1,0:T(8,128)(2,1)S(1)} %copy-done.3), custom_call_target="tpu_custom_call" | custom-call | tf_op jit(solution)/shard_map/pallas_call | solution.py:204
  52.4 0.8 %copy.10 = bf16[128,16,128]{2,1,0:T(8,128)(2,1)} copy(bf16[128,16,128]{2,1,0:T(8,128)(2,1)S(1)} %get-tuple-element.6) | data formatting | bytes 1048576
  53.2 0.8 %copy.11 = bf16[128,16,128]{2,1,0:T(8,128)(2,1)} copy(bf16[128,16,128]{2,1,0:T(8,128)(2,1)S(1)} %get-tuple-element.7) | data formatting | bytes 1048576
  54.0 0.8 %copy.12 = bf16[128,16,128]{2,1,0:T(8,128)(2,1)} copy(bf16[128,16,128]{2,1,0:T(8,128)(2,1)S(1)} %get-tuple-element.8) | data formatting | bytes 1048576
Async XLA Ops:
  0.6 1.0 %copy-start = (bf16[128,16,128]{2,1,0:T(8,128)(2,1)S(1)}, bf16[128,16,128]{2,1,0:T(8,128)(2,1)}, u32[]{:S(2)}) copy-start(bf16[128,16,128]{2,1,0:T(8,128)(2,1)} %q_ref.1) | copy-start | bytes 1572868
  1.7 1.0 %copy-start.1 = (bf16[128,16,128]{2,1,0:T(8,128)(2,1)S(1)}, bf16[128,16,128]{2,1,0:T(8,128)(2,1)}, u32[]{:S(2)}) copy-start(bf16[128,16,128]{2,1,0:T(8,128)(2,1)} %k_ref.1) | copy-start | bytes 1572868
  2.7 1.0 %copy-start.2 = (bf16[128,16,128]{2,1,0:T(8,128)(2,1)S(1)}, bf16[128,16,128]{2,1,0:T(8,128)(2,1)}, u32[]{:S(2)}) copy-start(bf16[128,16,128]{2,1,0:T(8,128)(2,1)} %v_ref.1) | copy-start | bytes 1572868
  3.8 1.0 %copy-start.3 = (bf16[128,16,128]{2,1,0:T(8,128)(2,1)S(1)}, bf16[128,16,128]{2,1,0:T(8,128)(2,1)}, u32[]{:S(2)}) copy-start(bf16[128,16,128]{2,1,0:T(8,128)(2,1)} %g_ref.1) | copy-start | bytes 1572868

commit v2 on v1

--- a/solution.py
+++ b/solution.py
@@ -8,7 +8,7 @@
 from jax.sharding import PartitionSpec as P
 
 MESH = pl.DeviceIdType.MESH
-GROUPS = 2
+GROUPS = 4
 
 PAIR, UP, ALONG, DOWN, BACK = range(5)
 
@@ -29,7 +29,7 @@
     dims, scale,
     q_ref, k_ref, v_ref, g_ref, dq_ref, dk_ref, dv_ref,
     qt, kt, vt, gt, acc, res, own, pair, chip, got, plane, along, down, base, back, final,
-    send, recv,
+    stage_in, load, send, recv,
 ):
     nz, nxy, groups = dims
     heads, tok, dim = qt.shape
@@ -44,6 +44,9 @@
     def there(dz, dxy, dcore):
         return (lax.rem(z + dz, nz), lax.rem(xy + dxy, nxy) * 2 + lax.rem(core + dcore, 2))
 
+    for i, src in enumerate((k_ref, v_ref, q_ref, g_ref)):
+        pltpu.make_async_copy(src, stage_in.at[i], load.at[i]).start()
+
     partners = [there(0, 0, 1)]
     partners += [there(0, k, 0) for k in range(1, nxy)]
     partners += [there(k, 0, 0) for k in range(1, nz)]
@@ -63,10 +66,9 @@
     def left(ref, stage, g):
         pltpu.make_async_copy(ref, ref, send.at[stage, g]).wait()
 
-    kt[...] = jnp.swapaxes(k_ref[...], 0, 1)
-    vt[...] = jnp.swapaxes(v_ref[...], 0, 1)
-    qt[...] = jnp.swapaxes(q_ref[...], 0, 1)
-    gt[...] = jnp.swapaxes(g_ref[...], 0, 1)
+    for i, (src, to) in enumerate(((k_ref, kt), (v_ref, vt), (q_ref, qt), (g_ref, gt))):
+        pltpu.make_async_copy(src, stage_in.at[i], load.at[i]).wait()
+        to[...] = jnp.swapaxes(stage_in[i], 0, 1)
 
     def states(g):
         for part in range(2):
@@ -76,7 +78,7 @@
                 own[g, part, 0, at] = tn(kt[h], vt[h])
                 own[g, part, 1, at] = tn(qt[h], gt[h])
                 return 0
-            lax.fori_loop(0, half, one, 0, unroll=2)
+            lax.fori_loop(0, half, one, 0, unroll=min(2, half))
 
     def pair_start(g):
         remote(own.at[g, 1 - core], pair.at[g], PAIR, g, there(0, 0, 1)).start()
@@ -153,7 +155,7 @@
             res[2, h] = (scale * (acc[2, h] + nn(kt[h], after))).astype(jnp.bfloat16)
             return 0
 
-        lax.fori_loop(0, half, one, 0, unroll=2)
+        lax.fori_loop(0, half, one, 0, unroll=min(2, half))
 
     def local_group(g):
         lax.fori_loop(g * per, (g + 1) * per, local, 0, unroll=2)
@@ -190,6 +192,14 @@
         left(back.at[g], BACK, g)
 
 
+def keep(a, b, c, oa, ob, oc, sems):
+    copies = [pltpu.make_async_copy(x, o, sems.at[i]) for i, (x, o) in enumerate(((a, oa), (b, ob), (c, oc)))]
+    for copy in copies:
+        copy.start()
+    for copy in copies:
+        copy.wait()
+
+
 def solution(mesh):
     nz, nxy = mesh.shape["outer"], mesh.shape["inner"] // 2
     groups = GROUPS
@@ -201,10 +211,10 @@
         r = rows // nxy
         f32, low = jnp.float32, jnp.bfloat16
         vmem = pl.BlockSpec(memory_space=pltpu.VMEM)
-        return pl.pallas_call(
+        grads = pl.pallas_call(
             functools.partial(kernel, (nz, nxy, groups), scale),
             out_shape=[jax.ShapeDtypeStruct((tok, heads, dim), low)] * 3,
-            in_specs=[vmem] * 4,
+            in_specs=[pl.BlockSpec(memory_space=pltpu.HBM)] * 4,
             out_specs=[vmem] * 3,
             scratch_shapes=[
                 pltpu.VMEM((heads, tok, dim), low),
@@ -223,13 +233,23 @@
                 pltpu.VMEM((groups, nxy, 2, r, dim), f32),
                 pltpu.VMEM((groups, 2, rows, dim), f32),
                 pltpu.VMEM((groups, 2, 2, rows, dim), f32),
+                pltpu.VMEM((4, tok, heads, dim), low),
+                pltpu.SemaphoreType.DMA((4,)),
                 pltpu.SemaphoreType.DMA((5, groups)),
                 pltpu.SemaphoreType.DMA((5, groups)),
             ],
             compiler_params=pltpu.CompilerParams(
-                collective_id=0, has_side_effects=True, vmem_limit_bytes=48 * 2**20
+                collective_id=0, has_side_effects=True, vmem_limit_bytes=54525952
             ),
         )(q, k, v, g)
+        return pl.pallas_call(
+            keep,
+            out_shape=[jax.ShapeDtypeStruct((tok, heads, dim), low)] * 3,
+            in_specs=[pl.BlockSpec(memory_space=pl.ANY)] * 3,
+            out_specs=[pl.BlockSpec(memory_space=pl.ANY)] * 3,
+            scratch_shapes=[pltpu.SemaphoreType.DMA((3,))],
+            compiler_params=pltpu.CompilerParams(vmem_limit_bytes=2**20),
+        )(*grads)
 
     spec = P(("outer", "inner"), None, None)
     return jax.shard_map(

time: 55.1 us -> 42.9 us (0.78)
  local copies, waits for them, and re-layouts: 6.54 us -> 0 us
  Pallas kernels: 47.6 us -> 42.1 us
    pallas_call x1, Pallas kernels: 47.6 us -> 41 us  [step(): pl.pallas_call(functools.partial(kernel, (nz, nxy, groups), scale), out_s...]
    unnamed x11 -> x0, local copies, waits for them, and re-layouts: 6.54 us -> none
    pallas_call x0 -> x1, Pallas kernels: none -> 1.17 us  [step(): pl.pallas_call(keep, out_shape=[jax.ShapeDtypeStruct((tok, heads, dim), l...]
where the time goes in v2:
time: 42.9 us; the launch traced here: 42.8 us
  Pallas kernels  42.1 us (98%)
  between operations  0.64 us (1%)
    pallas_call x1, Pallas kernels, step(): pl.pallas_call(functools.partial(kernel, (nz, nxy, groups), scale), out_s...  41 us
    pallas_call x1, Pallas kernels, step(): pl.pallas_call(keep, out_shape=[jax.ShapeDtypeStruct((tok, heads, dim), l...  1.17 us

profile of v2, /device:TPU:1, one launch (start us, length us, event | category | flops | bytes accessed | tf_op | source)
XLA Modules:
  0.0 42.8 jit_solution(8623493377974076077)
XLA Ops:
  0.6 41.0 %shard_map.67 = (bf16[128,16,128]{2,1,0:T(8,128)(2,1)S(1)}, bf16[128,16,128]{2,1,0:T(8,128)(2,1)S(1)}, bf16[128,16,128]{2,1,0:T(8,128)(2,1)S(1)}) custom-call(bf16[128,16,128]{2,1,0:T(8,128)(2,1)} %q_ref.1, bf16[128,16,128]{2,1,0:T(8,128)(2,1)} %k_ref.1, bf16[128,16,128]{2,1,0:T(8,128)(2,1)} %v_ref.1, bf16[128,16,128]{2,1,0:T(8,128)(2,1)} %g_ref.1), custom_call_target="tpu_custom_call" | custom-call | tf_op jit(solution)/shard_map/pallas_call | solution.py:214
  41.6 1.2 %shard_map.68 = (bf16[128,16,128]{2,1,0:T(8,128)(2,1)}, bf16[128,16,128]{2,1,0:T(8,128)(2,1)}, bf16[128,16,128]{2,1,0:T(8,128)(2,1)}) custom-call(bf16[128,16,128]{2,1,0:T(8,128)(2,1)S(1)} %get-tuple-element.6.a, bf16[128,16,128]{2,1,0:T(8,128)(2,1)S(1)} %get-tuple-element.7.b, bf16[128,16,128]{2,1,0:T(8,128)(2,1)S(1)} %get-tuple-element.8.c), custom_call_target="tpu_custom_call" | custom-call | tf_op jit(solution)/shard_map/pallas_call | solution.py:245

commit v3 on v0

v3 whole, which is shorter than its diff:
```python
import functools

import jax
import jax.numpy as jnp
from jax import lax
from jax.experimental import pallas as pl
from jax.experimental.pallas import tpu as pltpu
from jax.sharding import PartitionSpec as P

MESH = pl.DeviceIdType.MESH
SIZES = (8, 8)

PAIR, UP, DOWN, BACK = range(4)


def nn(a, b):
    return lax.dot_general(a, b, (((1,), (0,)), ((), ())), preferred_element_type=jnp.float32)


def nt(a, b):
    return lax.dot_general(a, b, (((1,), (1,)), ((), ())), preferred_element_type=jnp.float32)


def tn(a, b):
    return lax.dot_general(a, b, (((0,), (0,)), ((), ())), preferred_element_type=jnp.float32)


def spread(nxy):
    nx = max(n for n in range(1, nxy + 1) if n * n <= nxy and nxy % n == 0)
    ny = nxy // nx
    order = ((2, 2), (2, 1), (1, 2), (2, 3), (3, 2), (2, 0), (0, 2), (1, 1), (3, 3), (1, 3), (3, 1), (1, 0), (0, 1), (3, 0), (0, 3))
    if (nx, ny) != (4, 4):
        order = [(a, b) for a in range(nx) for b in range(ny) if a or b]
    return nx, ny, order


def unroll(count):
    return next(n for n in (4, 3, 2, 1) if count % n == 0)


def kernel(dims, scale, k_ref, v_ref, q_ref, g_ref, dq_ref, dk_ref, dv_ref, raw, low, acc, *rest):
    nz, nxy, sizes = dims
    count = len(sizes)
    load, send, recv, zsend, zrecv = rest[-5:]
    buffers = [rest[10 * i : 10 * i + 10] for i in range(count)]
    heads, tok, dim = acc.shape[1:]
    begins = [sum(sizes[:i]) for i in range(count)]
    z = lax.axis_index("outer")
    inner = lax.axis_index("inner")
    xy, core = inner // 2, inner % 2
    lead = jnp.where(z < nz // 2, 0, 1)

    def there(dz, dxy, dcore):
        return (lax.rem(z + dz, nz), lax.rem(xy + dxy, nxy) * 2 + lax.rem(core + dcore, 2))

    nx, ny, order = spread(nxy)
    x, y = xy // ny, xy % ny

    def across(a, b):
        if nx == ny:
            a, b = jnp.where(core == 0, a, b), jnp.where(core == 0, b, a)
        return lax.rem(x + a, nx) * ny + lax.rem(y + b, ny)

    def to_plane(src, dst, stage, n, s):
        for a, b in order:
            who = across(a, b)
            remote(src.at[s, who], dst.at[s, xy], stage, n, s, (z, who * 2 + core)).start()
        pltpu.make_async_copy(src.at[s, xy], dst.at[s, xy], recv.at[stage, n, s]).start()

    partners = [there(0, 0, 1)]
    partners += [there(0, k, 0) for k in range(1, nxy)]
    partners += [there(k, 0, 0) for k in range(1, nz)]
    barrier = pltpu.get_barrier_semaphore()
    for who in partners:
        pl.semaphore_signal(barrier, inc=1, device_id=who, device_id_type=MESH)

    inputs = (k_ref, v_ref, q_ref, g_ref)

    def fetch(i):
        pltpu.make_async_copy(inputs[i], raw.at[i], load.at[i]).start()

    @pl.when(lead == 0)
    def _():
        for i in (0, 1, 2, 3):
            fetch(i)

    @pl.when(lead == 1)
    def _():
        for i in (2, 3, 0, 1):
            fetch(i)

    def remote(src, dst, stage, n, s, who):
        return pltpu.make_async_remote_copy(
            src_ref=src, dst_ref=dst, send_sem=send.at[stage, n, s], recv_sem=recv.at[stage, n, s],
            device_id=who, device_id_type=MESH,
        )

    def arrived(ref, stage, n, s):
        pltpu.make_async_copy(ref, ref, recv.at[stage, n, s]).wait()

    def left(ref, stage, n, s):
        pltpu.make_async_copy(ref, ref, send.at[stage, n, s]).wait()

    def by_head(s, first, heads_now):
        for i in range(2):
            at = 2 * s + i
            if first == 0:
                pltpu.make_async_copy(raw.at[at], raw.at[at], load.at[at]).wait()
            some = pl.ds(first, heads_now)
            low[at, some] = jnp.swapaxes(raw[at, :, some], 0, 1)

    def states(n, s, part):
        own = buffers[n][0]
        half = sizes[n] // 2

        def one(j, _):
            h = begins[n] + part * half + j
            own[s, part, pl.ds(pl.multiple_of(j * dim, dim), dim)] = tn(low[2 * s, h], low[2 * s + 1, h])
            return 0

        lax.fori_loop(0, half, one, 0, unroll=unroll(half))

    def pair_start(n, s):
        own, pair = buffers[n][:2]
        states(n, s, 1 - core)
        if n == 0 and s is lead:
            pl.semaphore_wait(barrier, len(partners))
        remote(own.at[s, 1 - core], pair.at[s], PAIR, n, s, there(0, 0, 1)).start()
        states(n, s, core)

    def up_start(n, s):
        own, pair, chip, got = buffers[n][:4]
        arrived(pair.at[s], PAIR, n, s)
        chip[s] = (own[s, core] + pair[s]).reshape(chip.shape[1:])
        to_plane(chip, got, UP, n, s)

    def z_copy(n, s, j):
        plane, along = buffers[n][4:6]
        to = jnp.where(s == 0, z + 1 + j, z - 1 - j)
        return pltpu.make_async_remote_copy(
            src_ref=plane.at[s], dst_ref=along.at[s, j], send_sem=zsend.at[n, s, j], recv_sem=zrecv.at[n, s, j],
            device_id=(to, inner), device_id_type=MESH,
        )

    def z_targets(s):
        return jnp.where(s == 0, nz - 1 - z, z)

    def z_sources(s):
        return jnp.where(s == 0, z, nz - 1 - z)

    def along_start(n, s):
        got, plane = buffers[n][3:5]
        arrived(got.at[s], UP, n, s)
        plane[s] = jnp.sum(got[s], axis=0)
        targets = z_targets(s)

        def one(j, _):
            z_copy(n, s, targets - 1 - j).start()
            return 0

        lax.fori_loop(0, targets, one, 0)

    def down_start(n, s):
        _, _, _, got, plane, along, down, base = buffers[n][:8]

        def one(j, total):
            pltpu.make_async_copy(along.at[s, j], along.at[s, j], zrecv.at[n, s, j]).wait()
            return total + along[s, j]

        total = lax.fori_loop(0, z_sources(s), one, jnp.zeros(plane.shape[1:], jnp.float32))
        for i in range(nxy):
            at = jnp.where(s == 0, i, nxy - 1 - i)
            down[s, at] = total
            total = total + got[s, at]
        to_plane(down, base, DOWN, n, s)

    def back_start(n, s):
        own, pair, _, _, _, _, _, base, back, final = buffers[n]
        arrived(base.at[s], DOWN, n, s)
        second = core + s == 1
        sums = base[s].reshape(back.shape[1:])
        back[s] = sums + jnp.where(second, 0.0, own[s, core])
        remote(back.at[s], final.at[s, 1], BACK, n, s, there(0, 0, 1)).start()
        final[s, 0] = sums + jnp.where(second, pair[s], 0.0)

    def local(h, _):
        at = lax.broadcasted_iota(jnp.int32, (tok, tok), 0)
        to = lax.broadcasted_iota(jnp.int32, (tok, tok), 1)
        k, v, q, d = low[0, h], low[1, h], low[2, h], low[3, h]
        dprob = jnp.where(to <= at, nt(d, v), 0.0).astype(jnp.bfloat16)
        dprob_t = jnp.where(at <= to, nt(v, d), 0.0).astype(jnp.bfloat16)
        score_t = jnp.where(at <= to, nt(k, q), 0.0).astype(jnp.bfloat16)
        acc[0, h] = nn(dprob, k)
        acc[1, h] = nn(dprob_t, q)
        acc[2, h] = nn(score_t, d)
        return 0

    def finish(n, s, which):
        final = buffers[n][9]
        half = sizes[n] // 2
        part = core if which == 0 else 1 - core

        def place(j):
            return begins[n] + part * half + j, pl.ds(pl.multiple_of(j * dim, dim), dim)

        def query_part(j, _):
            h, at = place(j)
            state = final[0, which, at].astype(jnp.bfloat16)
            dq_ref[h] = (scale * (acc[0, h] + nt(low[3, h], state))).astype(jnp.bfloat16)
            return 0

        def key_value_part(j, _):
            h, at = place(j)
            state = final[1, which, at].astype(jnp.bfloat16)
            dk_ref[h] = (scale * (acc[1, h] + nt(low[1, h], state))).astype(jnp.bfloat16)
            dv_ref[h] = (scale * (acc[2, h] + nn(low[0, h], state))).astype(jnp.bfloat16)
            return 0

        @pl.when(s == 0)
        def _():
            lax.fori_loop(0, half, query_part, 0, unroll=unroll(half))

        @pl.when(s == 1)
        def _():
            lax.fori_loop(0, half, key_value_part, 0, unroll=unroll(half))

    def finish_other(n, s):
        arrived(buffers[n][9].at[s, 1], BACK, n, s)
        finish(n, s, 1)

    def drain(i):
        n, s = jobs[i]
        _, pair, chip, _, plane, _, down, _, _, _ = buffers[n]
        left(pair.at[s], PAIR, n, s)
        left(chip.at[s, pl.ds(0, nxy - 1)], UP, n, s)
        if i < last:
            left(down.at[s, pl.ds(0, nxy - 1)], DOWN, n, s)

        def one(j, _):
            pltpu.make_async_copy(plane.at[s], plane.at[s], zsend.at[n, s, j]).wait()
            return 0

        lax.fori_loop(0, z_targets(s), one, 0)

    other = 1 - lead
    jobs = [(n, lead) for n in range(count)] + [(n, other) for n in reversed(range(count))]
    last = len(jobs) - 1
    eight = heads // 2
    by_head(lead, 0, eight)
    pair_start(*jobs[0])
    by_head(lead, eight, eight)
    pair_start(*jobs[1])
    up_start(*jobs[0])
    by_head(other, 0, eight)
    by_head(other, eight, eight)
    for i in range(2, last + 1):
        pair_start(*jobs[i])
        up_start(*jobs[i - 1])
    up_start(*jobs[last])
    def local_part(i):
        begin, end = heads * i // last, heads * (i + 1) // last
        lax.fori_loop(begin, end, local, 0, unroll=unroll(end - begin))

    for i, job in enumerate(jobs):
        if i < last:
            local_part(i)
        along_start(*job)
        if i >= 1:
            down_start(*jobs[i - 1])
    down_start(*jobs[last])
    for i, job in enumerate(jobs):
        if i == last:
            for j in range(last + 1):
                drain(j)
        back_start(*job)
        if i >= 1:
            finish_other(*jobs[i - 1])
        finish(*job, 0)
    finish_other(*jobs[last])
    left(buffers[jobs[last][0]][6].at[jobs[last][1], pl.ds(0, nxy - 1)], DOWN, *jobs[last])
    for n, s in jobs:
        left(buffers[n][8].at[s], BACK, n, s)


def by_token(a, b, c, oa, ob, oc, turned, sems):
    copies = []
    for i, (x, o) in enumerate(((a, oa), (b, ob), (c, oc))):
        turned[i] = jnp.swapaxes(x[...], 0, 1)
        copies.append(pltpu.make_async_copy(turned.at[i], o, sems.at[i]))
        copies[-1].start()
    for copy in copies:
        copy.wait()


def solution(mesh):
    nz, nxy = mesh.shape["outer"], mesh.shape["inner"] // 2
    f32, bf16 = jnp.float32, jnp.bfloat16

    def step(q, k, v, g):
        tok, heads, dim = q.shape
        assert sum(SIZES) == heads
        scale = (dim * tok * mesh.size) ** -0.5
        scratch = [
            pltpu.VMEM((4, tok, heads, dim), bf16),
            pltpu.VMEM((4, heads, tok, dim), bf16),
            pltpu.VMEM((3, heads, tok, dim), f32),
        ]
        for size in SIZES:
            rows = size // 2 * dim
            r = rows // nxy
            scratch += [
                pltpu.VMEM((2, 2, rows, dim), f32),
                pltpu.VMEM((2, rows, dim), f32),
                pltpu.VMEM((2, nxy, r, dim), f32),
                pltpu.VMEM((2, nxy, r, dim), f32),
                pltpu.VMEM((2, r, dim), f32),
                pltpu.VMEM((2, nz - 1, r, dim), f32),
                pltpu.VMEM((2, nxy, r, dim), f32),
                pltpu.VMEM((2, nxy, r, dim), f32),
                pltpu.VMEM((2, rows, dim), f32),
                pltpu.VMEM((2, 2, rows, dim), f32),
            ]
        count = len(SIZES)
        scratch += [
            pltpu.SemaphoreType.DMA((4,)),
            pltpu.SemaphoreType.DMA((4, count, 2)),
            pltpu.SemaphoreType.DMA((4, count, 2)),
            pltpu.SemaphoreType.DMA((count, 2, nz - 1)),
            pltpu.SemaphoreType.DMA((count, 2, nz - 1)),
        ]
        vmem, hbm = pl.BlockSpec(memory_space=pltpu.VMEM), pl.BlockSpec(memory_space=pltpu.HBM)
        whole = pl.BlockSpec(memory_space=pl.ANY)
        grads = pl.pallas_call(
            functools.partial(kernel, (nz, nxy, SIZES), scale),
            out_shape=[jax.ShapeDtypeStruct((heads, tok, dim), bf16)] * 3,
            in_specs=[hbm] * 4,
            out_specs=[vmem] * 3,
            scratch_shapes=scratch,
            compiler_params=pltpu.CompilerParams(
                collective_id=0, has_side_effects=True, vmem_limit_bytes=52 * 2**20
            ),
        )(k, v, q, g)
        return pl.pallas_call(
            by_token,
            out_shape=[jax.ShapeDtypeStruct((tok, heads, dim), bf16)] * 3,
            in_specs=[vmem] * 3,
            out_specs=[whole] * 3,
            scratch_shapes=[pltpu.VMEM((3, tok, heads, dim), bf16), pltpu.SemaphoreType.DMA((3,))],
            compiler_params=pltpu.CompilerParams(vmem_limit_bytes=4 * 2**20),
        )(*grads)

    spec = P(("outer", "inner"), None, None)
    return jax.shard_map(
        step, mesh=mesh, in_specs=(spec,) * 4, out_specs=(spec,) * 3, check_vma=False
    )
```

time: 676 us -> 41.9 us (0.06)
  waiting for transfers between devices: 485 us -> 0 us
  other arithmetic: 151 us -> 0 us
  Pallas kernels: 0 us -> 41.1 us
  matrix products: 18.2 us -> 0 us
  between operations: 15.3 us -> 0.64 us
    all_gather x4 -> x0, waiting for transfers between devices: 292 us -> none  [carried_in(): everything = jax.tree.map(lambda part: lax.all_gather(part, axis), x)]
    psum x2 -> x0, waiting for transfers between devices: 190 us -> none  [the longest x1 119 us: carry_states(): totals = lax.psum((states[0], states[1]), 'inner')]
    select_n x40 -> x0, other arithmetic: 149 us -> none  [step(): return jax.tree.map(lambda a, b: jnp.where(reached, a, b), new, before)]
    pallas_call x0 -> x2, Pallas kernels: none -> 41.1 us  [the longest x1 39.8 us: step(): pl.pallas_call(functools.partial(kernel, (nz, nxy, SIZES), scale), out_sh...]
    dot_general x9 -> x0, matrix products: 18.2 us -> none  [the longest x1 2.69 us: body(): jnp.einsum('hts,thv->shv', score_low, output_gradient, preferred_element_...]
  transfers between devices with their start and end apart: 6 -> 0, of which waited for: 5 -> 0; matrix products, arithmetic and copies ran while one was open for 24% -> 0% of each run, Pallas kernels for 0% -> 0%
where the time goes in v3:
time: 41.9 us; the launch traced here: 41.8 us
  Pallas kernels  41.1 us (98%)
  between operations  0.64 us (2%)
    pallas_call x1, Pallas kernels, step(): pl.pallas_call(functools.partial(kernel, (nz, nxy, SIZES), scale), out_sh...  39.8 us
    pallas_call x1, Pallas kernels, step(): pl.pallas_call(by_token, out_shape=[jax.ShapeDtypeStruct((tok, heads, dim...  1.33 us

profile of v3, /device:TPU:1, one launch (start us, length us, event | category | flops | bytes accessed | tf_op | source)
XLA Modules:
  0.0 41.8 jit_solution(16364920006802932854)
XLA Ops:
  0.6 39.8 %shard_map.67 = (bf16[16,128,128]{2,1,0:T(8,128)(2,1)S(1)}, bf16[16,128,128]{2,1,0:T(8,128)(2,1)S(1)}, bf16[16,128,128]{2,1,0:T(8,128)(2,1)S(1)}) custom-call(bf16[128,16,128]{2,1,0:T(8,128)(2,1)} %k_ref.1, bf16[128,16,128]{2,1,0:T(8,128)(2,1)} %v_ref.1, bf16[128,16,128]{2,1,0:T(8,128)(2,1)} %q_ref.1, bf16[128,16,128]{2,1,0:T(8,128)(2,1)} %g_ref.1), custom_call_target="tpu_custom_call" | custom-call | tf_op jit(solution)/shard_map/pallas_call | solution.py:333
  40.4 1.3 %shard_map.68 = (bf16[128,16,128]{2,1,0:T(8,128)(2,1)}, bf16[128,16,128]{2,1,0:T(8,128)(2,1)}, bf16[128,16,128]{2,1,0:T(8,128)(2,1)}) custom-call(bf16[16,128,128]{2,1,0:T(8,128)(2,1)S(1)} %get-tuple-element.6.a, bf16[16,128,128]{2,1,0:T(8,128)(2,1)S(1)} %get-tuple-element.7.b, bf16[16,128,128]{2,1,0:T(8,128)(2,1)S(1)} %get-tuple-element.8.c), custom_call_target="tpu_custom_call" | custom-call | tf_op jit(solution)/shard_map/pallas_call | solution.py:343

commit v4 on v3

--- a/solution.py
+++ b/solution.py
@@ -9,6 +9,7 @@
 
 MESH = pl.DeviceIdType.MESH
 SIZES = (8, 8)
+BANDS = (2, 2, 4)
 
 PAIR, UP, DOWN, BACK = range(4)
 
@@ -67,12 +68,39 @@
             remote(src.at[s, who], dst.at[s, xy], stage, n, s, (z, who * 2 + core)).start()
         pltpu.make_async_copy(src.at[s, xy], dst.at[s, xy], recv.at[stage, n, s]).start()
 
-    partners = [there(0, 0, 1)]
-    partners += [there(0, k, 0) for k in range(1, nxy)]
-    partners += [there(k, 0, 0) for k in range(1, nz)]
+    bands = BANDS if nz == 8 else (nz // 2, nz - nz // 2)
+    edges = [sum(bands[:i]) for i in range(len(bands) + 1)]
+    low_edge = sum(jnp.where(z >= edge, edge - under, 0) for under, edge in zip(edges, edges[1:-1]))
+    high_edge = nz - sum(jnp.where(z < edge, above - edge, 0) for edge, above in zip(edges[1:-1], edges[2:]))
+
     barrier = pltpu.get_barrier_semaphore()
-    for who in partners:
+
+    def greet(who):
         pl.semaphore_signal(barrier, inc=1, device_id=who, device_id_type=MESH)
+
+    def greet_planes(begin, end):
+        def one(at, _):
+            @pl.when(at != z)
+            def _():
+                greet((at, inner))
+            return 0
+
+        lax.fori_loop(begin, end, one, 0)
+
+    greet(there(0, 0, 1))
+    for a, b in order:
+        greet((z, across(a, b) * 2 + core))
+    greet_planes(low_edge, high_edge)
+
+    def first_wait():
+        pl.semaphore_wait(barrier, nxy + high_edge - 1)
+        greet_planes(high_edge, nz)
+        greet_planes(0, low_edge)
+
+    def second_wait():
+        @pl.when(high_edge < nz)
+        def _():
+            pl.semaphore_wait(barrier, nz - high_edge)
 
     inputs = (k_ref, v_ref, q_ref, g_ref)
 
@@ -124,7 +152,7 @@
         own, pair = buffers[n][:2]
         states(n, s, 1 - core)
         if n == 0 and s is lead:
-            pl.semaphore_wait(barrier, len(partners))
+            first_wait()
         remote(own.at[s, 1 - core], pair.at[s], PAIR, n, s, there(0, 0, 1)).start()
         states(n, s, core)
 
@@ -264,6 +292,8 @@
     for i, job in enumerate(jobs):
         if i < last:
             local_part(i)
+        if i == 0:
+            second_wait()
         along_start(*job)
         if i >= 1:
             down_start(*jobs[i - 1])

time: 41.9 us -> 40.2 us (0.959)
  Pallas kernels: 41.1 us -> 39.4 us
    pallas_call x1, Pallas kernels: 39.8 us -> 38.1 us  [step(): pl.pallas_call(functools.partial(kernel, (nz, nxy, SIZES), scale), out_sh...]
where the time goes in v4:
time: 40.2 us; the launch traced here: 40.1 us
  Pallas kernels  39.4 us (98%)
  between operations  0.64 us (2%)
    pallas_call x1, Pallas kernels, step(): pl.pallas_call(functools.partial(kernel, (nz, nxy, SIZES), scale), out_sh...  38.1 us
    pallas_call x1, Pallas kernels, step(): pl.pallas_call(by_token, out_shape=[jax.ShapeDtypeStruct((tok, heads, dim...  1.33 us

profile of v4, /device:TPU:1, one launch (start us, length us, event | category | flops | bytes accessed | tf_op | source)
XLA Modules:
  0.0 40.1 jit_solution(16455783766692217363)
XLA Ops:
  0.6 38.1 %shard_map.67 = (bf16[16,128,128]{2,1,0:T(8,128)(2,1)S(1)}, bf16[16,128,128]{2,1,0:T(8,128)(2,1)S(1)}, bf16[16,128,128]{2,1,0:T(8,128)(2,1)S(1)}) custom-call(bf16[128,16,128]{2,1,0:T(8,128)(2,1)} %k_ref.1, bf16[128,16,128]{2,1,0:T(8,128)(2,1)} %v_ref.1, bf16[128,16,128]{2,1,0:T(8,128)(2,1)} %q_ref.1, bf16[128,16,128]{2,1,0:T(8,128)(2,1)} %g_ref.1), custom_call_target="tpu_custom_call" | custom-call | tf_op jit(solution)/shard_map/pallas_call | solution.py:363
  38.7 1.3 %shard_map.68 = (bf16[128,16,128]{2,1,0:T(8,128)(2,1)}, bf16[128,16,128]{2,1,0:T(8,128)(2,1)}, bf16[128,16,128]{2,1,0:T(8,128)(2,1)}) custom-call(bf16[16,128,128]{2,1,0:T(8,128)(2,1)S(1)} %get-tuple-element.6.a, bf16[16,128,128]{2,1,0:T(8,128)(2,1)S(1)} %get-tuple-element.7.b, bf16[16,128,128]{2,1,0:T(8,128)(2,1)S(1)} %get-tuple-element.8.c), custom_call_target="tpu_custom_call" | custom-call | tf_op jit(solution)/shard_map/pallas_call | solution.py:373

commit v5 on v4

--- a/solution.py
+++ b/solution.py
@@ -9,7 +9,7 @@
 
 MESH = pl.DeviceIdType.MESH
 SIZES = (8, 8)
-BANDS = (2, 2, 4)
+BANDS = (3, 5)
 
 PAIR, UP, DOWN, BACK = range(4)
 
@@ -49,7 +49,7 @@
     z = lax.axis_index("outer")
     inner = lax.axis_index("inner")
     xy, core = inner // 2, inner % 2
-    lead = jnp.where(z < nz // 2, 0, 1)
+    lead = jnp.where(z < 3, 0, 1)
 
     def there(dz, dxy, dcore):
         return (lax.rem(z + dz, nz), lax.rem(xy + dxy, nxy) * 2 + lax.rem(core + dcore, 2))

time: 40.2 us -> 39.2 us (0.975)
  Pallas kernels: 39.4 us -> 38.3 us
    pallas_call x1, Pallas kernels: 38.1 us -> 37 us  [step(): pl.pallas_call(functools.partial(kernel, (nz, nxy, SIZES), scale), out_sh...]
where the time goes in v5:
time: 39.2 us; the launch traced here: 39 us
  Pallas kernels  38.3 us (98%)
  between operations  0.64 us (2%)
    pallas_call x1, Pallas kernels, step(): pl.pallas_call(functools.partial(kernel, (nz, nxy, SIZES), scale), out_sh...  37 us
    pallas_call x1, Pallas kernels, step(): pl.pallas_call(by_token, out_shape=[jax.ShapeDtypeStruct((tok, heads, dim...  1.33 us

profile of v5, /device:TPU:1, one launch (start us, length us, event | category | flops | bytes accessed | tf_op | source)
XLA Modules:
  0.0 39.0 jit_solution(8761781431765704580)
XLA Ops:
  0.6 37.0 %shard_map.67 = (bf16[16,128,128]{2,1,0:T(8,128)(2,1)S(1)}, bf16[16,128,128]{2,1,0:T(8,128)(2,1)S(1)}, bf16[16,128,128]{2,1,0:T(8,128)(2,1)S(1)}) custom-call(bf16[128,16,128]{2,1,0:T(8,128)(2,1)} %k_ref.1, bf16[128,16,128]{2,1,0:T(8,128)(2,1)} %v_ref.1, bf16[128,16,128]{2,1,0:T(8,128)(2,1)} %q_ref.1, bf16[128,16,128]{2,1,0:T(8,128)(2,1)} %g_ref.1), custom_call_target="tpu_custom_call" | custom-call | tf_op jit(solution)/shard_map/pallas_call | solution.py:363
  37.7 1.3 %shard_map.68 = (bf16[128,16,128]{2,1,0:T(8,128)(2,1)}, bf16[128,16,128]{2,1,0:T(8,128)(2,1)}, bf16[128,16,128]{2,1,0:T(8,128)(2,1)}) custom-call(bf16[16,128,128]{2,1,0:T(8,128)(2,1)S(1)} %get-tuple-element.6.a, bf16[16,128,128]{2,1,0:T(8,128)(2,1)S(1)} %get-tuple-element.7.b, bf16[16,128,128]{2,1,0:T(8,128)(2,1)S(1)} %get-tuple-element.8.c), custom_call_target="tpu_custom_call" | custom-call | tf_op jit(solution)/shard_map/pallas_call | solution.py:373

commit v6 on v5

--- a/solution.py
+++ b/solution.py
@@ -313,11 +313,15 @@
 
 
 def by_token(a, b, c, oa, ob, oc, turned, sems):
+    parts = sems.shape[1]
+    rows = a.shape[1] // parts
     copies = []
     for i, (x, o) in enumerate(((a, oa), (b, ob), (c, oc))):
-        turned[i] = jnp.swapaxes(x[...], 0, 1)
-        copies.append(pltpu.make_async_copy(turned.at[i], o, sems.at[i]))
-        copies[-1].start()
+        for j in range(parts):
+            some = pl.ds(j * rows, rows)
+            turned[i, some] = jnp.swapaxes(x[:, some], 0, 1)
+            copies.append(pltpu.make_async_copy(turned.at[i, some], o.at[some], sems.at[i, j]))
+            copies[-1].start()
     for copy in copies:
         copy.wait()
 
@@ -375,7 +379,7 @@
             out_shape=[jax.ShapeDtypeStruct((tok, heads, dim), bf16)] * 3,
             in_specs=[vmem] * 3,
             out_specs=[whole] * 3,
-            scratch_shapes=[pltpu.VMEM((3, tok, heads, dim), bf16), pltpu.SemaphoreType.DMA((3,))],
+            scratch_shapes=[pltpu.VMEM((3, tok, heads, dim), bf16), pltpu.SemaphoreType.DMA((3, 2))],
             compiler_params=pltpu.CompilerParams(vmem_limit_bytes=4 * 2**20),
         )(*grads)
 

time: 39.2 us -> 39.1 us (level)
  no operation moved by 1% of the time
where the time goes in v6:
time: 39.1 us; the launch traced here: 38.9 us
  Pallas kernels  38.3 us (98%)
  between operations  0.64 us (2%)
    pallas_call x1, Pallas kernels, step(): pl.pallas_call(functools.partial(kernel, (nz, nxy, SIZES), scale), out_sh...  37 us
    pallas_call x1, Pallas kernels, step(): pl.pallas_call(by_token, out_shape=[jax.ShapeDtypeStruct((tok, heads, dim...  1.27 us

profile of v6, /device:TPU:1, one launch (start us, length us, event | category | flops | bytes accessed | tf_op | source)
XLA Modules:
  0.0 38.9 jit_solution(15788871392345399433)
XLA Ops:
  0.6 37.0 %shard_map.67 = (bf16[16,128,128]{2,1,0:T(8,128)(2,1)S(1)}, bf16[16,128,128]{2,1,0:T(8,128)(2,1)S(1)}, bf16[16,128,128]{2,1,0:T(8,128)(2,1)S(1)}) custom-call(bf16[128,16,128]{2,1,0:T(8,128)(2,1)} %k_ref.1, bf16[128,16,128]{2,1,0:T(8,128)(2,1)} %v_ref.1, bf16[128,16,128]{2,1,0:T(8,128)(2,1)} %q_ref.1, bf16[128,16,128]{2,1,0:T(8,128)(2,1)} %g_ref.1), custom_call_target="tpu_custom_call" | custom-call | tf_op jit(solution)/shard_map/pallas_call | solution.py:367
  37.7 1.3 %shard_map.68 = (bf16[128,16,128]{2,1,0:T(8,128)(2,1)}, bf16[128,16,128]{2,1,0:T(8,128)(2,1)}, bf16[128,16,128]{2,1,0:T(8,128)(2,1)}) custom-call(bf16[16,128,128]{2,1,0:T(8,128)(2,1)S(1)} %get-tuple-element.6.a, bf16[16,128,128]{2,1,0:T(8,128)(2,1)S(1)} %get-tuple-element.7.b, bf16[16,128,128]{2,1,0:T(8,128)(2,1)S(1)} %get-tuple-element.8.c), custom_call_target="tpu_custom_call" | custom-call | tf_op jit(solution)/shard_map/pallas_call | solution.py:377
